TPU v7x, 32 devices: a whole 2x2x4 slice. The times are simulated.
32 devices in a mesh: seq: 8 (over y, x, core), head: 4 (over z).
Axes of the slice: x: 2, y: 2, z: 4, core: 2. Of those that a mesh axis runs over, the one named last changes fastest.
Arguments:
- queries: bfloat16 [8192, 4096], P('seq', 'head'), may hold values from -6 to 6
- key_states: bfloat16 [8192, 2048], P('seq', 'head'), may hold values from -6 to 6
- value_states: bfloat16 [8192, 2048], P('seq', 'head'), may hold values from -6 to 6
- outputs: bfloat16 [8192, 4096], P('seq', 'head'), may hold values from -6 to 6
- out_grad: bfloat16 [8192, 4096], P(('seq', 'head')), may hold values from -96 to 96
- log_norm: float32 [32, 8192], P('head', 'seq'), may hold values from 6 to 7.6
Outputs:
- query_grad: bfloat16 [8192, 4096], P(('seq', 'head'))
- key_grad: bfloat16 [8192, 2048], P(('seq', 'head'))
- value_grad: bfloat16 [8192, 2048], P(('seq', 'head'))
All inputs are finite; a program needn't handle non-finite values.
Results may differ from a plain program's by a relative error of at most 0.0049.
Values may be sent and summed in bfloat16 or wider, within the bound.
A program may use at most 128 MiB of HBM per device.

v0:
```python
import jax
import jax.numpy as jnp
from jax import lax
from jax.sharding import PartitionSpec as P

HEAD_DIM = 128
WINDOW = 1024


score_scale = 168.0 ** (-0.5)


def from_behind(shard, axis, by):
    devices = lax.axis_size(axis)
    pairs = [(i, i + by) for i in range(devices) if 0 <= i + by < devices]
    return lax.ppermute(shard, axis, pairs)


def band_tile(
    q_rows, grad_rows, norm_rows, delta_rows, key_rows, value_rows, query_start, key_start
):
    row_count = q_rows.shape[0]
    key_count = key_rows.shape[0]
    key_heads = key_rows.shape[1] // HEAD_DIM
    query_heads = q_rows.shape[1] // HEAD_DIM
    group_size = query_heads // key_heads
    query_split = q_rows.reshape(row_count, key_heads, group_size, HEAD_DIM)
    grad_split = grad_rows.reshape(row_count, key_heads, group_size, HEAD_DIM)
    key_split = key_rows.reshape(key_count, key_heads, HEAD_DIM)
    value_split = value_rows.reshape(key_count, key_heads, HEAD_DIM)
    scores = (
        jnp.einsum("qhgd,khd->hgqk", query_split, key_split, preferred_element_type=jnp.float32)
        * score_scale
    )
    query_pos = query_start + lax.broadcasted_iota(jnp.int32, (row_count, key_count), 0)
    key_pos = key_start + lax.broadcasted_iota(jnp.int32, (row_count, key_count), 1)
    offset_gap = query_pos - key_pos
    allowed = (offset_gap >= 0) & (offset_gap < WINDOW) & (key_pos >= 0)
    norm_split = norm_rows.reshape(key_heads, group_size, row_count)
    delta_split = delta_rows.reshape(key_heads, group_size, row_count)
    probability = jnp.where(allowed, jnp.exp(scores - norm_split[..., None]), 0.0)
    probs_low = probability.astype(jnp.bfloat16)
    grad_prob = jnp.einsum(
        "qhgd,khd->hgqk", grad_split, value_split, preferred_element_type=jnp.float32
    )
    grad_score = (probability * (grad_prob - delta_split[..., None])).astype(jnp.bfloat16)
    grad_q = (
        jnp.einsum("hgqk,khd->qhgd", grad_score, key_split, preferred_element_type=jnp.float32)
        * score_scale
    )
    grad_k = (
        jnp.einsum("hgqk,qhgd->khd", grad_score, query_split, preferred_element_type=jnp.float32)
        * score_scale
    )
    grad_v = jnp.einsum("hgqk,qhgd->khd", probs_low, grad_split, preferred_element_type=jnp.float32)
    return (
        grad_q.reshape(row_count, query_heads * HEAD_DIM),
        grad_k.reshape(key_count, key_heads * HEAD_DIM),
        grad_v.reshape(key_count, key_heads * HEAD_DIM),
    )


def on_device(queries, key_states, value_states, outputs, out_grad, log_norm):
    local_tokens = queries.shape[0]
    query_heads = queries.shape[1] // HEAD_DIM
    key_width = key_states.shape[1]
    block_rows = min(512, local_tokens)
    block_count = local_tokens // block_rows
    span_rows = WINDOW + block_rows
    base_pos = lax.axis_index("seq") * local_tokens
    grad_local = lax.all_to_all(out_grad, "head", split_axis=1, concat_axis=0, tiled=True)
    grad_delta = jnp.einsum(
        "qhd,qhd->hq",
        grad_local.reshape(local_tokens, query_heads, HEAD_DIM),
        outputs.reshape(local_tokens, query_heads, HEAD_DIM),
        preferred_element_type=jnp.float32,
    )
    key_rim, value_rim = from_behind((key_states, value_states), "seq", 1)
    key_ext = jnp.concatenate([key_rim, key_states], 0)
    value_ext = jnp.concatenate([value_rim, value_states], 0)

    def one_block(block_index, carried):
        grad_q_all, grad_k_all, grad_v_all = carried
        row_start = block_index * block_rows
        q_rows = lax.dynamic_slice_in_dim(queries, row_start, block_rows, 0)
        grad_rows = lax.dynamic_slice_in_dim(grad_local, row_start, block_rows, 0)
        norm_rows = lax.dynamic_slice_in_dim(log_norm, row_start, block_rows, 1)
        delta_rows = lax.dynamic_slice_in_dim(grad_delta, row_start, block_rows, 1)
        key_rows = lax.dynamic_slice_in_dim(key_ext, row_start, span_rows, 0)
        value_rows = lax.dynamic_slice_in_dim(value_ext, row_start, span_rows, 0)
        grad_q, grad_k, grad_v = band_tile(
            q_rows,
            grad_rows,
            norm_rows,
            delta_rows,
            key_rows,
            value_rows,
            base_pos + row_start,
            base_pos + row_start - WINDOW,
        )
        grad_q_all = lax.dynamic_update_slice_in_dim(
            grad_q_all, grad_q.astype(jnp.bfloat16), row_start, 0
        )
        old_k = lax.dynamic_slice_in_dim(grad_k_all, row_start, span_rows, 0)
        old_v = lax.dynamic_slice_in_dim(grad_v_all, row_start, span_rows, 0)
        grad_k_all = lax.dynamic_update_slice_in_dim(grad_k_all, old_k + grad_k, row_start, 0)
        grad_v_all = lax.dynamic_update_slice_in_dim(grad_v_all, old_v + grad_v, row_start, 0)
        return (grad_q_all, grad_k_all, grad_v_all)

    initial = (
        jnp.zeros((local_tokens, queries.shape[1]), jnp.bfloat16),
        jnp.zeros((WINDOW + local_tokens, key_width), jnp.float32),
        jnp.zeros((WINDOW + local_tokens, key_width), jnp.float32),
    )
    grad_q_all, grad_k_all, grad_v_all = lax.fori_loop(0, block_count, one_block, initial)
    rim_k, rim_v = from_behind((grad_k_all[:WINDOW], grad_v_all[:WINDOW]), "seq", -1)
    own_k = grad_k_all[WINDOW:].at[local_tokens - WINDOW :].add(rim_k).astype(jnp.bfloat16)
    own_v = grad_v_all[WINDOW:].at[local_tokens - WINDOW :].add(rim_v).astype(jnp.bfloat16)
    query_grad, key_grad, value_grad = (
        lax.all_to_all(grad_q_all, "head", split_axis=0, concat_axis=1, tiled=True),
        lax.all_to_all(own_k, "head", split_axis=0, concat_axis=1, tiled=True),
        lax.all_to_all(own_v, "head", split_axis=0, concat_axis=1, tiled=True),
    )
    return (query_grad, key_grad, value_grad)


def solution(mesh):
    placed = (
        P("seq", "head"),
        P("seq", "head"),
        P("seq", "head"),
        P("seq", "head"),
        P(("seq", "head"), None),
        P("head", "seq"),
    )
    return jax.shard_map(
        on_device,
        mesh=mesh,
        in_specs=placed,
        out_specs=(P(("seq", "head"), None), P(("seq", "head"), None), P(("seq", "head"), None)),
        check_vma=False,
    )
```

profile of v0, /device:TPU:0, one launch (start us, length us, event | category | flops | bytes accessed | tf_op | source)
XLA Modules:
  0.0 336.5 jit_solution(8833313606605791057)
XLA Ops:
  0.6 4.1 %copy.62 = bf16[256,4096]{0,1:T(8,128)(2,1)} copy(bf16[256,4096]{1,0:T(8,128)(2,1)} %param.20) | data formatting | bytes 4194304 | tf_op args[4]
  4.7 6.4 %all-to-all-start = ((bf16[256,4,1024]{0,2,1:T(8,128)(2,1)}), bf16[256,4,1024]{0,2,1:T(8,128)(2,1)S(1)}, u32[]{:S(2)}, u32[]{:S(2)}) async-start(bf16[256,4,1024]{0,2,1:T(8,128)(2,1)} %bitcast.122), calls=%async_computation | async-start | bytes 4194304 | tf_op jit(solution)/shard_map/all_to_all | solution.py:71
  16.4 4.0 %collective-permute-start.1 = (bf16[1024,512]{0,1:T(8,128)(2,1)S(1)}, bf16[1024,512]{0,1:T(8,128)(2,1)}, u32[]{:S(2)}, u32[]{:S(2)}) collective-permute-start(bf16[1024,512]{0,1:T(8,128)(2,1)S(1)} %copy.60), channel_id=1, source_target_pairs={{0,4},{4,8},{8,12},{12,16},{16,20},{20,24},{24,28},{1,5},{5,9},{9,... | collective-permute-start | bytes 3145736 | tf_op jit(solution)/shard_map/ppermute | solution.py:16
  20.4 3.6 %copy.102 = bf16[128,8,8,128]{3,2,1,0:T(8,128)(2,1)} copy(bf16[128,8,8,128]{3,1,2,0:T(8,128)(2,1)} %bitcast.131) | data formatting | bytes 4194304
  29.8 29.6 %all-to-all-done = bf16[256,4,1024]{0,2,1:T(8,128)(2,1)S(1)} async-done(((bf16[256,4,1024]{0,2,1:T(8,128)(2,1)}), bf16[256,4,1024]{0,2,1:T(8,128)(2,1)S(1)}, u32[]{:S(2)}, u32[]{:S(2)}) %all-to-all-start) | async-done | bytes 2097184 | tf_op jit(solution)/shard_map/all_to_all | solution.py:71
  72.1 153.0 %while.23 = (s32[]{:T(128)}, bf16[1024,1024]{1,0:T(8,128)(2,1)}, f32[2048,512]{0,1:T(8,128)}, f32[2048,512]{0,1:T(8,128)}, bf16[2048,512]{0,1:T(8,128)(2,1)}, /*...) while((s32[]{:T(128)}, bf16[1024,1024]{1,0:T(8,128)(2,1)}, ...), condition=%wide.region_1.2_spmd, body=%wide.region_0.1_spmd.sunk | while | flops 8104449024 | bytes 225627600 | solution.py:115
  79.3 11.5 %fusion.45 = f32[4,2,512,1536]{2,3,1,0:T(8,128)} fusion(bf16[1536,4,128,1]{0,2,3,1:T(8,128)(2,1)S(1)} %bitcast.117, bf16[512,4,2,128]{0,3,2,1:T(8,128)(2,1)S(1)} %bitcast.119, f32[4,2,512]{2,1,0:T(2,128)S(1)} %sub.114, pred[512,1536]{0,1:T(8,128)(4,1)S(1)} %fusion.44), kind=kOutput, calls=%fused_computation.5.clone.1 | convolution fusion | flops 1629487104 | bytes 28590080 | tf_op jit(solution)/shard_map/while/body/eval_jaxpr/qhgd,khd->hgqk/dot_general | solution.py:32
  94.8 14.9 %fusion.46 = bf16[4,2,512,1536]{2,3,1,0:T(8,128)(2,1)} fusion(f32[4,2,512,1536]{2,3,1,0:T(8,128)} %fusion.45, bf16[1536,4,128,1]{0,2,3,1:T(8,128)(2,1)S(1)} %bitcast.116, bf16[512,4,2,128]{0,3,2,1:T(8,128)(2,1)S(1)} %bitcast.114, f32[4,2,512]{2,1,0:T(2,128)S(1)} %sub.116), kind=kOutput, calls=%fused_computation.2.clone.1 | convolution fusion | flops 1629487104 | bytes 40386560 | tf_op jit(solution)/shard_map/while/body/eval_jaxpr/qhgd,khd->hgqk/dot_general | solution.py:43
  109.7 7.8 %multiply_convert_fusion.2 = bf16[4,128,2,512]{3,1,2,0:T(8,128)(2,1)} fusion(bf16[1536,4,128,1]{0,2,3,1:T(8,128)(2,1)} %bitcast.118, bf16[4,2,512,1536]{2,3,1,0:T(8,128)(2,1)} %fusion.46), kind=kOutput, calls=%fused_computation.16.clone.1 | convolution fusion | flops 1611661312 | bytes 15204352 | tf_op jit(solution)/shard_map/while/body/eval_jaxpr/hgqk,khd->qhgd/dot_general | solution.py:48
  120.1 12.8 %fusion.47 = f32[4,128,1536,1]{2,1,3,0:T(8,128)S(1)} fusion(bf16[512,4,2,128]{0,3,2,1:T(8,128)(2,1)} %bitcast.115, f32[4,2,512,1536]{2,3,1,0:T(8,128)} %fusion.45), kind=kOutput, calls=%fused_computation.6.clone.1 | convolution fusion | flops 1616904192 | bytes 29360128 | tf_op jit(solution)/shard_map/while/body/eval_jaxpr/hgqk,qhgd->khd/dot_general | solution.py:55
  132.9 9.2 %fusion.48 = f32[4,128,1536]{2,1,0:T(8,128)S(1)} fusion(bf16[512,4,2,128]{0,3,2,1:T(8,128)(2,1)} %bitcast.120, bf16[4,2,512,1536]{2,3,1,0:T(8,128)(2,1)} %fusion.46), kind=kOutput, calls=%fused_computation.11.clone.1 | convolution fusion | flops 1611399168 | bytes 16777216 | tf_op jit(solution)/shard_map/while/body/eval_jaxpr/hgqk,qhgd->khd/dot_general | solution.py:52
  142.0 4.5 %constant_dynamic-update-slice_fusion.6 = (f32[2048,512]{0,1:T(8,128)}, f32[2048,512]{0,1:T(8,128)S(1)}) fusion(f32[2048,512]{0,1:T(8,128)} %get-tuple-element.463, s32[]{:T(128)S(6)} %select_n.45, f32[4,128,1536,1]{2,1,3,0:T(8,128)S(1)} %fusion.47, f32[2048,512]{0,1:T(8,128)S(1)} %copy-done.2, f32[4,128,1536]{2,1,0:T(8,128)S(1)} %fusion.48), kind=kLoop, calls=%fused_computation.19.clone.1 | loop fusion | flops 1572864 | bytes 18874372 | tf_op jit(solution)/shard_map/while/body/eval_jaxpr/dynamic_update_slice | solution.py:107
  155.7 11.6 %fusion.45 = f32[4,2,512,1536]{2,3,1,0:T(8,128)} fusion(bf16[1536,4,128,1]{0,2,3,1:T(8,128)(2,1)S(1)} %bitcast.117, bf16[512,4,2,128]{0,3,2,1:T(8,128)(2,1)S(1)} %bitcast.119, f32[4,2,512]{2,1,0:T(2,128)S(1)} %sub.114, pred[512,1536]{0,1:T(8,128)(4,1)S(1)} %fusion.44), kind=kOutput, calls=%fused_computation.5.clone.1 | convolution fusion | flops 1629487104 | bytes 28590080 | tf_op jit(solution)/shard_map/while/body/eval_jaxpr/qhgd,khd->hgqk/dot_general | solution.py:32
  171.3 14.9 %fusion.46 = bf16[4,2,512,1536]{2,3,1,0:T(8,128)(2,1)} fusion(f32[4,2,512,1536]{2,3,1,0:T(8,128)} %fusion.45, bf16[1536,4,128,1]{0,2,3,1:T(8,128)(2,1)S(1)} %bitcast.116, bf16[512,4,2,128]{0,3,2,1:T(8,128)(2,1)S(1)} %bitcast.114, f32[4,2,512]{2,1,0:T(2,128)S(1)} %sub.116), kind=kOutput, calls=%fused_computation.2.clone.1 | convolution fusion | flops 1629487104 | bytes 40386560 | tf_op jit(solution)/shard_map/while/body/eval_jaxpr/qhgd,khd->hgqk/dot_general | solution.py:43
  186.2 7.8 %multiply_convert_fusion.2 = bf16[4,128,2,512]{3,1,2,0:T(8,128)(2,1)} fusion(bf16[1536,4,128,1]{0,2,3,1:T(8,128)(2,1)} %bitcast.118, bf16[4,2,512,1536]{2,3,1,0:T(8,128)(2,1)} %fusion.46), kind=kOutput, calls=%fused_computation.16.clone.1 | convolution fusion | flops 1611661312 | bytes 15204352 | tf_op jit(solution)/shard_map/while/body/eval_jaxpr/hgqk,khd->qhgd/dot_general | solution.py:48
  196.5 12.8 %fusion.47 = f32[4,128,1536,1]{2,1,3,0:T(8,128)S(1)} fusion(bf16[512,4,2,128]{0,3,2,1:T(8,128)(2,1)} %bitcast.115, f32[4,2,512,1536]{2,3,1,0:T(8,128)} %fusion.45), kind=kOutput, calls=%fused_computation.6.clone.1 | convolution fusion | flops 1616904192 | bytes 29360128 | tf_op jit(solution)/shard_map/while/body/eval_jaxpr/hgqk,qhgd->khd/dot_general | solution.py:55
  209.3 9.2 %fusion.48 = f32[4,128,1536]{2,1,0:T(8,128)S(1)} fusion(bf16[512,4,2,128]{0,3,2,1:T(8,128)(2,1)} %bitcast.120, bf16[4,2,512,1536]{2,3,1,0:T(8,128)(2,1)} %fusion.46), kind=kOutput, calls=%fused_computation.11.clone.1 | convolution fusion | flops 1611399168 | bytes 16777216 | tf_op jit(solution)/shard_map/while/body/eval_jaxpr/hgqk,qhgd->khd/dot_general | solution.py:52
  218.5 4.6 %constant_dynamic-update-slice_fusion.6 = (f32[2048,512]{0,1:T(8,128)}, f32[2048,512]{0,1:T(8,128)S(1)}) fusion(f32[2048,512]{0,1:T(8,128)} %get-tuple-element.463, s32[]{:T(128)S(6)} %select_n.45, f32[4,128,1536,1]{2,1,3,0:T(8,128)S(1)} %fusion.47, f32[2048,512]{0,1:T(8,128)S(1)} %copy-done.2, f32[4,128,1536]{2,1,0:T(8,128)S(1)} %fusion.48), kind=kLoop, calls=%fused_computation.19.clone.1 | loop fusion | flops 1572864 | bytes 18874372 | tf_op jit(solution)/shard_map/while/body/eval_jaxpr/dynamic_update_slice | solution.py:107
  225.1 3.6 %all-to-all-start.1 = ((bf16[4,256,1024]{2,1,0:T(8,128)(2,1)}), bf16[4,256,1024]{2,1,0:T(8,128)(2,1)S(1)}, u32[]{:S(2)}, u32[]{:S(2)}) async-start(bf16[4,256,1024]{2,1,0:T(8,128)(2,1)} %bitcast.124), calls=%async_computation.1 | async-start | bytes 4194304 | tf_op jit(solution)/shard_map/all_to_all | solution.py:120
  238.7 37.6 %all-to-all-done.1 = bf16[4,256,1024]{2,1,0:T(8,128)(2,1)S(1)} async-done(((bf16[4,256,1024]{2,1,0:T(8,128)(2,1)}), bf16[4,256,1024]{2,1,0:T(8,128)(2,1)S(1)}, u32[]{:S(2)}, u32[]{:S(2)}) %all-to-all-start.1) | async-done | bytes 2097184 | tf_op jit(solution)/shard_map/all_to_all | solution.py:120
  276.3 4.3 %all-to-all-start.2 = ((bf16[4,256,512]{2,1,0:T(8,128)(2,1)}), bf16[4,256,512]{2,1,0:T(8,128)(2,1)}, u32[]{:S(2)}, u32[]{:S(2)}) async-start(bf16[4,256,512]{2,1,0:T(8,128)(2,1)} %bitcast.127), calls=%async_computation.2 | async-start | bytes 2097152 | tf_op jit(solution)/shard_map/all_to_all | solution.py:121
  284.5 21.4 %all-to-all-done.2 = bf16[4,256,512]{2,1,0:T(8,128)(2,1)} async-done(((bf16[4,256,512]{2,1,0:T(8,128)(2,1)}), bf16[4,256,512]{2,1,0:T(8,128)(2,1)}, u32[]{:S(2)}, u32[]{:S(2)}) %all-to-all-start.2) | async-done | bytes 1048608 | tf_op jit(solution)/shard_map/all_to_all | solution.py:121
  312.0 4.1 %copy.72 = bf16[256,4096]{1,0:T(8,128)(2,1)} copy(bf16[256,4096]{0,1:T(8,128)(2,1)} %bitcast.126) | data formatting | bytes 4194304
  319.0 15.6 %all-to-all-done.3 = bf16[4,256,512]{2,1,0:T(8,128)(2,1)S(1)} async-done(((bf16[4,256,512]{2,1,0:T(8,128)(2,1)}), bf16[4,256,512]{2,1,0:T(8,128)(2,1)S(1)}, u32[]{:S(2)}, u32[]{:S(2)}) %all-to-all-start.3) | async-done | bytes 1048608 | tf_op jit(solution)/shard_map/all_to_all | solution.py:122
  (96 shorter events, 79.6 us)
Async XLA Ops:
  4.7 6.5 %copy-start.9 = (bf16[1024,512]{1,0:T(8,128)(2,1)S(1)}, bf16[1024,512]{1,0:T(8,128)(2,1)}, u32[]{:S(2)}) copy-start(bf16[1024,512]{1,0:T(8,128)(2,1)} %param.17) | copy-start | bytes 3145732
  4.7 54.6 %all-to-all-start = ((bf16[256,4,1024]{0,2,1:T(8,128)(2,1)}), bf16[256,4,1024]{0,2,1:T(8,128)(2,1)S(1)}, u32[]{:S(2)}, u32[]{:S(2)}) async-start(bf16[256,4,1024]{0,2,1:T(8,128)(2,1)} %bitcast.122), calls=%async_computation | async-start | bytes 4194304 | tf_op jit(solution)/shard_map/all_to_all | solution.py:71
  12.5 11.5 %collective-permute-start = (bf16[1024,512]{0,1:T(8,128)(2,1)}, bf16[1024,512]{0,1:T(8,128)(2,1)}, u32[]{:S(2)}, u32[]{:S(2)}) collective-permute-start(bf16[1024,512]{0,1:T(8,128)(2,1)} %copy.58), channel_id=1, source_target_pairs={{0,4},{4,8},{8,12},{12,16},{16,20},{20,24},{24,28},{1,5},{5,9},{9,... | collective-permute-start | bytes 3145736 | tf_op jit(solution)/shard_map/ppermute | solution.py:16
  16.4 10.6 %collective-permute-start.1 = (bf16[1024,512]{0,1:T(8,128)(2,1)S(1)}, bf16[1024,512]{0,1:T(8,128)(2,1)}, u32[]{:S(2)}, u32[]{:S(2)}) collective-permute-start(bf16[1024,512]{0,1:T(8,128)(2,1)S(1)} %copy.60), channel_id=1, source_target_pairs={{0,4},{4,8},{8,12},{12,16},{16,20},{20,24},{24,28},{1,5},{5,9},{9,... | collective-permute-start | bytes 3145736 | tf_op jit(solution)/shard_map/ppermute | solution.py:16
  61.8 2.4 copy-start.8
  69.6 2.5 copy-start.10
  73.6 17.2 %copy-start.1 = (bf16[1536,512]{0,1:T(8,128)(2,1)}, bf16[1536,512]{0,1:T(8,128)(2,1)S(1)}, u32[]{:S(2)}) copy-start(bf16[1536,512]{0,1:T(8,128)(2,1)S(1)} %constant_dynamic-slice_fusion.12) | copy-start | bytes 4718596 | tf_op jit(solution)/shard_map/while
  77.9 12.9 %copy-start.6 = (bf16[512,1024]{0,1:T(8,128)(2,1)}, bf16[512,1024]{0,1:T(8,128)(2,1)S(1)}, u32[]{:S(2)}) copy-start(bf16[512,1024]{0,1:T(8,128)(2,1)S(1)} %copy.106) | copy-start | bytes 3145732 | tf_op jit(solution)/shard_map/while
  79.2 11.6 %copy-start.7 = (bf16[2048,512]{0,1:T(8,128)(2,1)S(1)}, bf16[2048,512]{0,1:T(8,128)(2,1)}, u32[]{:S(2)}) copy-start(bf16[2048,512]{0,1:T(8,128)(2,1)} %get-tuple-element.485) | copy-start | bytes 6291460 | tf_op jit(solution)/shard_map/while
  94.7 15.0 %copy-start = (bf16[512,1024]{0,1:T(8,128)(2,1)}, bf16[512,1024]{0,1:T(8,128)(2,1)S(1)}, u32[]{:S(2)}) copy-start(bf16[512,1024]{0,1:T(8,128)(2,1)S(1)} %copy.107) | copy-start | bytes 3145732 | tf_op jit(solution)/shard_map/while
  132.8 9.2 %copy-start.2 = (f32[2048,512]{0,1:T(8,128)S(1)}, f32[2048,512]{0,1:T(8,128)}, u32[]{:S(2)}) copy-start(f32[2048,512]{0,1:T(8,128)} %get-tuple-element.462) | copy-start | bytes 12582916 | tf_op jit(solution)/shard_map/while
  146.6 2.0 copy-start.3
  150.1 17.2 %copy-start.1 = (bf16[1536,512]{0,1:T(8,128)(2,1)}, bf16[1536,512]{0,1:T(8,128)(2,1)S(1)}, u32[]{:S(2)}) copy-start(bf16[1536,512]{0,1:T(8,128)(2,1)S(1)} %constant_dynamic-slice_fusion.12) | copy-start | bytes 4718596 | tf_op jit(solution)/shard_map/while
  154.4 12.9 %copy-start.6 = (bf16[512,1024]{0,1:T(8,128)(2,1)}, bf16[512,1024]{0,1:T(8,128)(2,1)S(1)}, u32[]{:S(2)}) copy-start(bf16[512,1024]{0,1:T(8,128)(2,1)S(1)} %copy.106) | copy-start | bytes 3145732 | tf_op jit(solution)/shard_map/while
  155.7 11.6 %copy-start.7 = (bf16[2048,512]{0,1:T(8,128)(2,1)S(1)}, bf16[2048,512]{0,1:T(8,128)(2,1)}, u32[]{:S(2)}) copy-start(bf16[2048,512]{0,1:T(8,128)(2,1)} %get-tuple-element.485) | copy-start | bytes 6291460 | tf_op jit(solution)/shard_map/while
  171.2 15.0 %copy-start = (bf16[512,1024]{0,1:T(8,128)(2,1)}, bf16[512,1024]{0,1:T(8,128)(2,1)S(1)}, u32[]{:S(2)}) copy-start(bf16[512,1024]{0,1:T(8,128)(2,1)S(1)} %copy.107) | copy-start | bytes 3145732 | tf_op jit(solution)/shard_map/while
  209.3 9.2 %copy-start.2 = (f32[2048,512]{0,1:T(8,128)S(1)}, f32[2048,512]{0,1:T(8,128)}, u32[]{:S(2)}) copy-start(f32[2048,512]{0,1:T(8,128)} %get-tuple-element.462) | copy-start | bytes 12582916 | tf_op jit(solution)/shard_map/while
  225.1 51.3 %all-to-all-start.1 = ((bf16[4,256,1024]{2,1,0:T(8,128)(2,1)}), bf16[4,256,1024]{2,1,0:T(8,128)(2,1)S(1)}, u32[]{:S(2)}, u32[]{:S(2)}) async-start(bf16[4,256,1024]{2,1,0:T(8,128)(2,1)} %bitcast.124), calls=%async_computation.1 | async-start | bytes 4194304 | tf_op jit(solution)/shard_map/all_to_all | solution.py:120
  228.7 3.5 %copy-start.5 = (f32[2048,512]{0,1:T(8,128)S(1)}, f32[2048,512]{0,1:T(8,128)}, u32[]{:S(2)}) copy-start(f32[2048,512]{0,1:T(8,128)} %get-tuple-element.311) | copy-start | bytes 12582916
  230.6 6.3 %copy-start.4 = (f32[2048,512]{0,1:T(8,128)S(1)}, f32[2048,512]{0,1:T(8,128)}, u32[]{:S(2)}) copy-start(f32[2048,512]{0,1:T(8,128)} %get-tuple-element.310) | copy-start | bytes 12582916
  230.6 6.3 %collective-permute-start.2 = (f32[1024,512]{0,1:T(8,128)S(1)}, f32[1024,512]{0,1:T(8,128)S(1)}, u32[]{:S(2)}, u32[]{:S(2)}) collective-permute-start(f32[1024,512]{0,1:T(8,128)S(1)} %slice.41), channel_id=1, source_target_pairs={{4,0},{8,4},{12,8},{16,12},{20,16},{24,20},{28,24},{5,1},{9,5},{13... | collective-permute-start | bytes 6291464 | tf_op jit(solution)/shard_map/ppermute | solution.py:16
  233.6 47.0 %collective-permute-start.3 = (f32[1024,512]{0,1:T(8,128)}, f32[1024,512]{0,1:T(8,128)}, u32[]{:S(2)}, u32[]{:S(2)}) collective-permute-start(f32[1024,512]{0,1:T(8,128)} %slice.43), channel_id=1, source_target_pairs={{4,0},{8,4},{12,8},{16,12},{20,16},{24,20},{28,24},{5,1},{9,5},{13... | collective-permute-start | bytes 6291464 | tf_op jit(solution)/shard_map/ppermute | solution.py:16
  276.3 29.5 %all-to-all-start.2 = ((bf16[4,256,512]{2,1,0:T(8,128)(2,1)}), bf16[4,256,512]{2,1,0:T(8,128)(2,1)}, u32[]{:S(2)}, u32[]{:S(2)}) async-start(bf16[4,256,512]{2,1,0:T(8,128)(2,1)} %bitcast.127), calls=%async_computation.2 | async-start | bytes 2097152 | tf_op jit(solution)/shard_map/all_to_all | solution.py:121
  305.9 28.7 %all-to-all-start.3 = ((bf16[4,256,512]{2,1,0:T(8,128)(2,1)}), bf16[4,256,512]{2,1,0:T(8,128)(2,1)S(1)}, u32[]{:S(2)}, u32[]{:S(2)}) async-start(bf16[4,256,512]{2,1,0:T(8,128)(2,1)} %bitcast.128), calls=%async_computation.3 | async-start | bytes 2097152 | tf_op jit(solution)/shard_map/all_to_all | solution.py:122
  (1 other events, 2.0 us)
where the time goes:
time: 338 us; the launch traced here: 337 us
  matrix products  112 us (33%)
  waiting for transfers between devices  106 us (31%)
  local copies, waits for them, and re-layouts  68 us (20%)
  starting transfers between devices  27.1 us (8%)
  other arithmetic  21.6 us (6%)
    all_to_all x1, waiting for transfers between devices, on_device(): lax.all_to_all(grad_q_all, 'head', split_axis=0, concat_axis=1, tiled=True)  37.6 us
    dot_general x2, matrix products, band_tile(): jnp.einsum('qhgd,khd->hgqk', grad_split, value_split, preferred_element_t...  29.8 us
    all_to_all x1, waiting for transfers between devices, on_device(): lax.all_to_all(out_grad, 'head', split_axis=1, concat_axis=0, tiled=True)  29.6 us
    dot_general x2, matrix products, band_tile(): jnp.einsum('hgqk,qhgd->khd', probs_low, grad_split, preferred_element_typ...  25.5 us
    dot_general x2, matrix products, band_tile(): jnp.einsum('qhgd,khd->hgqk', query_split, key_split, preferred_element_ty...  23.1 us
    all_to_all x1, waiting for transfers between devices, on_device(): lax.all_to_all(own_k, 'head', split_axis=0, concat_axis=1, tiled=True)  21.4 us
    unnamed x18, local copies, waits for them, and re-layouts  19.7 us
    dot_general x2, matrix products, band_tile(): jnp.einsum('hgqk,qhgd->khd', grad_score, query_split, preferred_element_t...  18.4 us
  transfers between devices with their start and end apart: 8, of which 5 were waited for; matrix products, arithmetic and copies ran while one was open for 9% of the time, Pallas kernels for 0%

commit v1 on v0

v1 whole, which is shorter than its diff:
```python
import functools
import math

import jax
import jax.numpy as jnp
from jax import lax
from jax.experimental import pallas as pl
from jax.experimental.pallas import tpu as pltpu
from jax.sharding import PartitionSpec as P

HEAD_DIM = 128
WINDOW = 1024
BLOCK = 256
AHEAD = 2

score_scale = 168.0 ** (-0.5)
LOG2E = math.log2(math.e)
MESH = pl.DeviceIdType.MESH


def at(start, size, step=None):
    return pl.ds(pl.multiple_of(start, size if step is None else step), size)


def dot(a, b, dims):
    return lax.dot_general(a, b, (dims, ((), ())), preferred_element_type=jnp.float32)


def kernel(
    seqs, heads, groups, ratio, tokens,
    q_hbm, k_hbm, v_hbm, o_hbm, g_hbm, n_hbm,
    dq_hbm, dk_hbm, dv_hbm,
    q_buf, o_buf, g_buf, k_ext, v_ext, norm, stats, k_turned, dq_turned,
    sums, rims, dq_buf, dkv_buf,
    in_sem, norm_sem, g_send, g_recv, kv_send, kv_recv, rim_send, rim_recv,
    dq_send, dq_recv, dkv_send, dkv_recv,
):
    s, z = lax.axis_index("seq"), lax.axis_index("head")
    owned = tokens // heads
    pair = ratio * HEAD_DIM
    q_blocks, rim_blocks = tokens // BLOCK, WINDOW // BLOCK
    has_before, has_after = s > 0, s < seqs - 1

    def inputs(g):
        wide, narrow = at(g * pair, pair), at(g * HEAD_DIM, HEAD_DIM)
        own = pl.ds(WINDOW, tokens)
        return [
            pltpu.make_async_copy(q_hbm.at[:, wide], q_buf.at[g], in_sem.at[g, 0]),
            pltpu.make_async_copy(o_hbm.at[:, wide], o_buf.at[g], in_sem.at[g, 1]),
            pltpu.make_async_copy(k_hbm.at[:, narrow], k_ext.at[g, own], in_sem.at[g, 2]),
            pltpu.make_async_copy(v_hbm.at[:, narrow], v_ext.at[g, own], in_sem.at[g, 3]),
            pltpu.make_async_copy(
                g_hbm.at[:, at(z * groups * pair + g * pair, pair)],
                g_buf.at[g, at(z * owned, owned)],
                in_sem.at[g, 4],
            ),
        ]

    def grad_in(g, d):
        peer = lax.rem(z + d, heads)
        return pltpu.make_async_remote_copy(
            src_ref=g_hbm.at[:, at(peer * groups * pair + g * pair, pair)],
            dst_ref=g_buf.at[g, at(z * owned, owned)],
            send_sem=g_send.at[g, d],
            recv_sem=g_recv.at[g, d],
            device_id={"head": peer},
            device_id_type=MESH,
        )

    def window_in(g, c):
        src, dst = ((k_hbm, k_ext), (v_hbm, v_ext))[c]
        return pltpu.make_async_remote_copy(
            src_ref=src.at[pl.ds(tokens - WINDOW, WINDOW), at(g * HEAD_DIM, HEAD_DIM)],
            dst_ref=dst.at[g, pl.ds(0, WINDOW)],
            send_sem=kv_send.at[g, c],
            recv_sem=kv_recv.at[g, c],
            device_id={"seq": s + 1},
            device_id_type=MESH,
        )

    def rim_out(g):
        return pltpu.make_async_remote_copy(
            src_ref=sums.at[g, :, pl.ds(0, WINDOW)],
            dst_ref=rims.at[g],
            send_sem=rim_send.at[g],
            recv_sem=rim_recv.at[g],
            device_id={"seq": s - 1},
            device_id_type=MESH,
        )

    def dq_out(g, d):
        peer = lax.rem(z + d, heads)
        return pltpu.make_async_remote_copy(
            src_ref=dq_buf.at[g, at(peer * owned, owned)],
            dst_ref=dq_hbm.at[:, at(z * groups * pair + g * pair, pair)],
            send_sem=dq_send.at[g, d],
            recv_sem=dq_recv.at[g, d],
            device_id={"head": peer},
            device_id_type=MESH,
        )

    def dq_own(g):
        return pltpu.make_async_copy(
            dq_buf.at[g, at(z * owned, owned)],
            dq_hbm.at[:, at(z * groups * pair + g * pair, pair)],
            dq_send.at[g, 0],
        )

    def dkv_out(g, c, d):
        peer = lax.rem(z + d, heads)
        return pltpu.make_async_remote_copy(
            src_ref=dkv_buf.at[g, c, at(peer * owned, owned)],
            dst_ref=(dk_hbm, dv_hbm)[c].at[:, at((z * groups + g) * HEAD_DIM, HEAD_DIM)],
            send_sem=dkv_send.at[g, c, d],
            recv_sem=dkv_recv.at[g, c, d],
            device_id={"head": peer},
            device_id_type=MESH,
        )

    def dkv_own(g, c):
        return pltpu.make_async_copy(
            dkv_buf.at[g, c, at(z * owned, owned)],
            (dk_hbm, dv_hbm)[c].at[:, at((z * groups + g) * HEAD_DIM, HEAD_DIM)],
            dkv_send.at[g, c, 0],
        )

    def send_grads(g):
        for d in range(1, heads):
            grad_in(g, d).start()

    def send_windows(g):
        @pl.when(has_after)
        def _():
            for c in range(2):
                window_in(g, c).start()

    def tile(g, j, i, in_rim):
        keys, rows = at(j * BLOCK, BLOCK), at(i * BLOCK, BLOCK)
        k_rows, v_rows, k_cols = k_ext[g, keys, :], v_ext[g, keys, :], k_turned[:, keys]
        ahead = lax.broadcasted_iota(jnp.int32, (BLOCK, BLOCK), 1) - lax.broadcasted_iota(
            jnp.int32, (BLOCK, BLOCK), 0
        )
        allowed = None
        if in_rim or q_blocks > rim_blocks:
            allowed = ahead < jnp.where(i < j, BLOCK, 0)
        if not in_rim:
            later = ahead >= jnp.where(i > j - rim_blocks, -BLOCK, 0)
            allowed = later if allowed is None else allowed & later
        dk = dv = None
        for h in range(ratio):
            lanes = slice(h * HEAD_DIM, (h + 1) * HEAD_DIM)
            q_rows, g_rows = q_buf[g, rows, lanes], g_buf[g, rows, lanes]
            scores = dot(k_rows, q_rows, ((1,), (1,)))
            probs = jnp.exp2(scores * (score_scale * LOG2E) - stats[h : h + 1, rows])
            probs = jnp.where(allowed, probs, 0.0)
            grad_prob = dot(v_rows, g_rows, ((1,), (1,)))
            grad_score = (
                probs * (grad_prob - stats[ratio + h : ratio + h + 1, rows])
            ).astype(jnp.bfloat16)
            dv_h = dot(probs.astype(jnp.bfloat16), g_rows, ((1,), (0,)))
            dk_h = dot(grad_score, q_rows, ((1,), (0,)))
            dq_turned[h, :, rows] += dot(k_cols, grad_score, ((1,), (0,)))
            dk = dk_h if dk is None else dk + dk_h
            dv = dv_h if dv is None else dv + dv_h
        sums[g, 0, keys, :] += dk
        sums[g, 1, keys, :] += dv

    def key_block(g, j, in_rim):
        keys = at(j * BLOCK, BLOCK)
        k_turned[:, keys] = k_ext[g, keys, :].astype(jnp.float32).T.astype(jnp.bfloat16)
        sums[g, :, keys, :] = jnp.zeros((2, BLOCK, HEAD_DIM), jnp.float32)
        low, high = jnp.maximum(j - rim_blocks, 0), jnp.minimum(j + 1, q_blocks)
        lax.fori_loop(low, high, lambda i, _: (tile(g, j, i, in_rim), 0)[1], 0)

    def prepare(g):
        ones = jnp.ones((8, HEAD_DIM), jnp.bfloat16)
        for h in range(ratio):
            lanes = slice(h * HEAD_DIM, (h + 1) * HEAD_DIM)
            stats[h : h + 1, :] = norm[pl.ds(g * ratio + h, 1), :] * LOG2E

            def rows_of(i, _, h=h, lanes=lanes):
                rows = at(i * BLOCK, BLOCK)
                both = g_buf[g, rows, lanes].astype(jnp.float32) * o_buf[g, rows, lanes].astype(
                    jnp.float32
                )
                high = both.astype(jnp.bfloat16)
                low = (both - high.astype(jnp.float32)).astype(jnp.bfloat16)
                delta = dot(ones, high, ((1,), (1,))) + dot(ones, low, ((1,), (1,)))
                stats[ratio + h : ratio + h + 1, rows] = delta[0:1, :]
                return 0

            lax.fori_loop(0, q_blocks, rows_of, 0)
            dq_turned[h] = jnp.zeros((HEAD_DIM, tokens), jnp.float32)

    def finish_dq(g):
        def rows_of(i, _):
            rows = at(i * BLOCK, BLOCK)
            for h in range(ratio):
                lanes = slice(h * HEAD_DIM, (h + 1) * HEAD_DIM)
                dq_buf[g, rows, lanes] = (dq_turned[h, :, rows].T * score_scale).astype(
                    jnp.bfloat16
                )
            return 0

        lax.fori_loop(0, q_blocks, rows_of, 0)
        for d in range(1, heads):
            dq_out(g, d).start()
        dq_own(g).start()

    def finish_dkv(g):
        @pl.when(has_after)
        def _():
            rim_out(g).wait_recv()

            def add(i, _):
                rows = at(i * BLOCK, BLOCK)
                own = at(tokens + i * BLOCK, BLOCK)
                for c in range(2):
                    sums[g, c, own, :] += rims[g, c, rows, :]
                return 0

            lax.fori_loop(0, rim_blocks, add, 0)

        def rows_of(i, _):
            rows, own = at(i * BLOCK, BLOCK), at(WINDOW + i * BLOCK, BLOCK)
            dkv_buf[g, 0, rows, :] = (sums[g, 0, own, :] * score_scale).astype(jnp.bfloat16)
            dkv_buf[g, 1, rows, :] = sums[g, 1, own, :].astype(jnp.bfloat16)
            return 0

        lax.fori_loop(0, q_blocks, rows_of, 0)
        for c in range(2):
            for d in range(1, heads):
                dkv_out(g, c, d).start()
            dkv_own(g, c).start()

    norm_in = pltpu.make_async_copy(n_hbm, norm, norm_sem)
    norm_in.start()

    def start_inputs(g, _):
        for copy in inputs(g):
            copy.start()
        return 0

    lax.fori_loop(0, groups, start_inputs, 0)

    barrier = pltpu.get_barrier_semaphore()
    for d in range(1, heads):
        pl.semaphore_signal(
            barrier, inc=1, device_id={"head": lax.rem(z + d, heads)}, device_id_type=MESH
        )

    @pl.when(has_before)
    def _():
        pl.semaphore_signal(barrier, inc=1, device_id={"seq": s - 1}, device_id_type=MESH)

    @pl.when(has_after)
    def _():
        pl.semaphore_signal(barrier, inc=1, device_id={"seq": s + 1}, device_id_type=MESH)

    pl.semaphore_wait(
        barrier, heads - 1 + has_before.astype(jnp.int32) + has_after.astype(jnp.int32)
    )

    for g in range(min(AHEAD, groups)):
        send_grads(g)
        send_windows(g)
    norm_in.wait()

    def one_group(g, _):
        for copy in inputs(g):
            copy.wait()
        for d in range(1, heads):
            grad_in(g, d).wait_recv()

        @pl.when(g + AHEAD < groups)
        def _():
            send_grads(g + AHEAD)
            send_windows(g + AHEAD)

        prepare(g)

        @pl.when(has_before)
        def _():
            for c in range(2):
                window_in(g, c).wait_recv()
            lax.fori_loop(0, rim_blocks, lambda j, _: (key_block(g, j, True), 0)[1], 0)
            rim_out(g).start()

        lax.fori_loop(
            rim_blocks, rim_blocks + q_blocks, lambda j, _: (key_block(g, j, False), 0)[1], 0
        )
        finish_dq(g)

        @pl.when(g > 0)
        def _():
            finish_dkv(g - 1)

        return 0

    lax.fori_loop(0, groups, one_group, 0)
    finish_dkv(groups - 1)

    def drain(g, _):
        for d in range(1, heads):
            grad_in(g, d).wait_send()
            dq_out(g, d).wait()
            for c in range(2):
                dkv_out(g, c, d).wait()
        dq_own(g).wait()
        for c in range(2):
            dkv_own(g, c).wait()

        @pl.when(has_after)
        def _():
            for c in range(2):
                window_in(g, c).wait_send()

        @pl.when(has_before)
        def _():
            rim_out(g).wait_send()

        return 0

    lax.fori_loop(0, groups, drain, 0)


def on_device(seqs, heads, queries, key_states, value_states, outputs, out_grad, log_norm):
    tokens = queries.shape[0]
    groups = key_states.shape[1] // HEAD_DIM
    ratio = queries.shape[1] // key_states.shape[1]
    pair, owned, span = ratio * HEAD_DIM, tokens // heads, WINDOW + tokens
    low, wide = jnp.bfloat16, jnp.float32
    dma = pltpu.SemaphoreType.DMA
    pairs = groups * ratio * tokens * (WINDOW + BLOCK)
    return pl.pallas_call(
        functools.partial(kernel, seqs, heads, groups, ratio, tokens),
        out_shape=(
            jax.ShapeDtypeStruct((owned, out_grad.shape[1]), low),
            jax.ShapeDtypeStruct((owned, key_states.shape[1] * heads), low),
            jax.ShapeDtypeStruct((owned, key_states.shape[1] * heads), low),
        ),
        in_specs=[pl.BlockSpec(memory_space=pl.ANY)] * 6,
        out_specs=[pl.BlockSpec(memory_space=pl.ANY)] * 3,
        scratch_shapes=[
            pltpu.VMEM((groups, tokens, pair), low),
            pltpu.VMEM((groups, tokens, pair), low),
            pltpu.VMEM((groups, tokens, pair), low),
            pltpu.VMEM((groups, span, HEAD_DIM), low),
            pltpu.VMEM((groups, span, HEAD_DIM), low),
            pltpu.VMEM(log_norm.shape, wide),
            pltpu.VMEM((2 * ratio, tokens), wide),
            pltpu.VMEM((HEAD_DIM, span), low),
            pltpu.VMEM((ratio, HEAD_DIM, tokens), wide),
            pltpu.VMEM((groups, 2, span, HEAD_DIM), wide),
            pltpu.VMEM((groups, 2, WINDOW, HEAD_DIM), wide),
            pltpu.VMEM((groups, tokens, pair), low),
            pltpu.VMEM((groups, 2, tokens, HEAD_DIM), low),
            dma((groups, 5)),
            dma,
            dma((groups, heads)),
            dma((groups, heads)),
            dma((groups, 2)),
            dma((groups, 2)),
            dma((groups,)),
            dma((groups,)),
            dma((groups, heads)),
            dma((groups, heads)),
            dma((groups, 2, heads)),
            dma((groups, 2, heads)),
        ],
        cost_estimate=pl.CostEstimate(
            flops=10 * pairs * HEAD_DIM, bytes_accessed=12 * tokens * 1024, transcendentals=pairs
        ),
        compiler_params=pltpu.CompilerParams(
            collective_id=0, has_side_effects=True, vmem_limit_bytes=56 * 1024 * 1024
        ),
    )(queries, key_states, value_states, outputs, out_grad, log_norm)


def solution(mesh):
    placed = (
        P("seq", "head"),
        P("seq", "head"),
        P("seq", "head"),
        P("seq", "head"),
        P(("seq", "head"), None),
        P("head", "seq"),
    )
    return jax.shard_map(
        functools.partial(on_device, mesh.shape["seq"], mesh.shape["head"]),
        mesh=mesh,
        in_specs=placed,
        out_specs=(P(("seq", "head"), None), P(("seq", "head"), None), P(("seq", "head"), None)),
        check_vma=False,
    )
```

time: 338 us -> 149 us (0.44)
  Pallas kernels: 0 us -> 143 us
  matrix products: 112 us -> 0 us
  waiting for transfers between devices: 106 us -> 0 us
  local copies, waits for them, and re-layouts: 68 us -> 5.79 us
  starting transfers between devices: 27.1 us -> 0 us
  other arithmetic: 21.6 us -> 0 us
    pallas_call x0 -> x1, Pallas kernels: none -> 143 us  [on_device(): pl.pallas_call(functools.partial(kernel, seqs, heads, groups, ratio, toke...]
    dot_general x10 -> x0, matrix products: 112 us -> none  [the longest x2 29.8 us: band_tile(): jnp.einsum('qhgd,khd->hgqk', grad_split, value_split, preferred_element_t...]
    all_to_all x4 -> x0, waiting for transfers between devices: 104 us -> none  [the longest x1 37.6 us: on_device(): lax.all_to_all(grad_q_all, 'head', split_axis=0, concat_axis=1, tiled=True)]
    dynamic_slice x16 -> x0, local copies, waits for them, and re-layouts: 19.5 us -> none  [the longest x4 8.65 us: one_block(): q_rows = lax.dynamic_slice_in_dim(queries, row_start, block_rows, 0)]
    all_to_all x4 -> x0, starting transfers between devices: 17.8 us -> none  [the longest x1 6.45 us: on_device(): lax.all_to_all(out_grad, 'head', split_axis=1, concat_axis=0, tiled=True)]
    unnamed x18 -> x7, local copies, waits for them, and re-layouts: 19.7 us -> 5.79 us
    ppermute x4 -> x0, starting transfers between devices: 9.25 us -> none  [from_behind(): return lax.ppermute(shard, axis, pairs)]
    dynamic_update_slice x2 -> x0, other arithmetic: 9.08 us -> none  [one_block(): lax.dynamic_update_slice_in_dim(grad_v_all, old_v + grad_v, row_start, 0)]
  transfers between devices with their start and end apart: 8 -> 0, of which waited for: 5 -> 0; matrix products, arithmetic and copies ran while one was open for 9% -> 0% of each run, Pallas kernels for 0% -> 0%
where the time goes in v1:
time: 149 us
  Pallas kernels  143 us (96%)
  local copies, waits for them, and re-layouts  5.79 us (4%)
    pallas_call x1, Pallas kernels, on_device(): pl.pallas_call(functools.partial(kernel, seqs, heads, groups, ratio, toke...  143 us
    unnamed x7, local copies, waits for them, and re-layouts  5.79 us

profile of v1, /device:TPU:0, one launch (start us, length us, event | category | flops | bytes accessed | tf_op | source)
XLA Modules:
  0.0 149.2 jit_solution(9675046992964469444)
XLA Ops:
  0.6 142.7 %shard_map.85 = (bf16[256,4096]{1,0:T(8,128)(2,1)}, bf16[256,2048]{1,0:T(8,128)(2,1)}, bf16[256,2048]{1,0:T(8,128)(2,1)}) custom-call(bf16[1024,1024]{1,0:T(8,128)(2,1)} %q_hbm.1, bf16[1024,512]{1,0:T(8,128)(2,1)} %k_hbm.1, bf16[1024,512]{1,0:T(8,128)(2,1)} %v_hbm.1, bf16[1024,1024]{1,0:T(8,128)(2,1)} %o_hbm.1, bf16[256,4096]{1,0:T(8,128)(2,1)} %g_hbm.1, ...), custom_call_target="tpu_custom_call" | custom-call | flops 13421772800 | bytes 12582912 | tf_op jit(solution)/shard_map/pallas_call | solution.py:335
  143.4 0.0 copy-start.1
  143.4 3.2 %copy.12 = bf16[256,4096]{1,0:T(8,128)(2,1)} copy(bf16[256,4096]{1,0:T(8,128)(2,1)} %get-tuple-element.6) | data formatting | bytes 4194304
  146.6 0.0 copy-done.1
  146.6 0.0 copy-start
  146.6 1.0 copy.13
  147.6 0.6 copy-done
  148.2 1.0 copy.14
Async XLA Ops:
  143.4 3.2 %copy-start.1 = (bf16[256,2048]{1,0:T(8,128)(2,1)S(1)}, bf16[256,2048]{1,0:T(8,128)(2,1)}, u32[]{:S(2)}) copy-start(bf16[256,2048]{1,0:T(8,128)(2,1)} %get-tuple-element.7) | copy-start | bytes 3145732
  146.6 1.6 %copy-start = (bf16[256,2048]{1,0:T(8,128)(2,1)S(1)}, bf16[256,2048]{1,0:T(8,128)(2,1)}, u32[]{:S(2)}) copy-start(bf16[256,2048]{1,0:T(8,128)(2,1)} %get-tuple-element.8) | copy-start | bytes 3145732

commit v2 on v1

--- a/solution.py
+++ b/solution.py
@@ -41,6 +41,17 @@
     q_blocks, rim_blocks = tokens // BLOCK, WINDOW // BLOCK
     has_before, has_after = s > 0, s < seqs - 1
 
+    in_low = (2 * z < heads).astype(jnp.int32)
+
+    def peer_of(n):
+        down, up = heads - 1 - n, jnp.int32(n)
+        down -= (down <= z).astype(jnp.int32)
+        up += (up >= z).astype(jnp.int32)
+        return in_low * down + (1 - in_low) * up
+
+    peers = [peer_of(n) for n in range(heads - 1)]
+    mine = heads - 1
+
     def inputs(g):
         wide, narrow = at(g * pair, pair), at(g * HEAD_DIM, HEAD_DIM)
         own = pl.ds(WINDOW, tokens)
@@ -56,13 +67,13 @@
             ),
         ]
 
-    def grad_in(g, d):
-        peer = lax.rem(z + d, heads)
+    def grad_in(g, n, source=None):
+        peer = peers[n]
         return pltpu.make_async_remote_copy(
             src_ref=g_hbm.at[:, at(peer * groups * pair + g * pair, pair)],
             dst_ref=g_buf.at[g, at(z * owned, owned)],
-            send_sem=g_send.at[g, d],
-            recv_sem=g_recv.at[g, d],
+            send_sem=g_send.at[g, n],
+            recv_sem=g_recv.at[g, z if source is None else source],
             device_id={"head": peer},
             device_id_type=MESH,
         )
@@ -88,13 +99,13 @@
             device_id_type=MESH,
         )
 
-    def dq_out(g, d):
-        peer = lax.rem(z + d, heads)
+    def dq_out(g, n, source=None):
+        peer = peers[n]
         return pltpu.make_async_remote_copy(
             src_ref=dq_buf.at[g, at(peer * owned, owned)],
             dst_ref=dq_hbm.at[:, at(z * groups * pair + g * pair, pair)],
-            send_sem=dq_send.at[g, d],
-            recv_sem=dq_recv.at[g, d],
+            send_sem=dq_send.at[g, n],
+            recv_sem=dq_recv.at[g, z if source is None else source],
             device_id={"head": peer},
             device_id_type=MESH,
         )
@@ -103,16 +114,16 @@
         return pltpu.make_async_copy(
             dq_buf.at[g, at(z * owned, owned)],
             dq_hbm.at[:, at(z * groups * pair + g * pair, pair)],
-            dq_send.at[g, 0],
-        )
-
-    def dkv_out(g, c, d):
-        peer = lax.rem(z + d, heads)
+            dq_send.at[g, mine],
+        )
+
+    def dkv_out(g, c, n, source=None):
+        peer = peers[n]
         return pltpu.make_async_remote_copy(
             src_ref=dkv_buf.at[g, c, at(peer * owned, owned)],
             dst_ref=(dk_hbm, dv_hbm)[c].at[:, at((z * groups + g) * HEAD_DIM, HEAD_DIM)],
-            send_sem=dkv_send.at[g, c, d],
-            recv_sem=dkv_recv.at[g, c, d],
+            send_sem=dkv_send.at[g, c, n],
+            recv_sem=dkv_recv.at[g, c, z if source is None else source],
             device_id={"head": peer},
             device_id_type=MESH,
         )
@@ -121,12 +132,12 @@
         return pltpu.make_async_copy(
             dkv_buf.at[g, c, at(z * owned, owned)],
             (dk_hbm, dv_hbm)[c].at[:, at((z * groups + g) * HEAD_DIM, HEAD_DIM)],
-            dkv_send.at[g, c, 0],
+            dkv_send.at[g, c, mine],
         )
 
     def send_grads(g):
-        for d in range(1, heads):
-            grad_in(g, d).start()
+        for n in range(heads - 1):
+            grad_in(g, n).start()
 
     def send_windows(g):
         @pl.when(has_after)
@@ -203,8 +214,8 @@
             return 0
 
         lax.fori_loop(0, q_blocks, rows_of, 0)
-        for d in range(1, heads):
-            dq_out(g, d).start()
+        for n in range(heads - 1):
+            dq_out(g, n).start()
         dq_own(g).start()
 
     def finish_dkv(g):
@@ -228,9 +239,10 @@
             return 0
 
         lax.fori_loop(0, q_blocks, rows_of, 0)
+        for n in range(heads - 1):
+            for c in range(2):
+                dkv_out(g, c, n).start()
         for c in range(2):
-            for d in range(1, heads):
-                dkv_out(g, c, d).start()
             dkv_own(g, c).start()
 
     norm_in = pltpu.make_async_copy(n_hbm, norm, norm_sem)
@@ -269,8 +281,8 @@
     def one_group(g, _):
         for copy in inputs(g):
             copy.wait()
-        for d in range(1, heads):
-            grad_in(g, d).wait_recv()
+        for n in range(heads - 1):
+            grad_in(g, n, peers[n]).wait_recv()
 
         @pl.when(g + AHEAD < groups)
         def _():
@@ -286,26 +298,25 @@
             lax.fori_loop(0, rim_blocks, lambda j, _: (key_block(g, j, True), 0)[1], 0)
             rim_out(g).start()
 
+        @pl.when(g > 0)
+        def _():
+            finish_dkv(g - 1)
+
         lax.fori_loop(
             rim_blocks, rim_blocks + q_blocks, lambda j, _: (key_block(g, j, False), 0)[1], 0
         )
         finish_dq(g)
-
-        @pl.when(g > 0)
-        def _():
-            finish_dkv(g - 1)
-
         return 0
 
     lax.fori_loop(0, groups, one_group, 0)
     finish_dkv(groups - 1)
 
     def drain(g, _):
-        for d in range(1, heads):
-            grad_in(g, d).wait_send()
-            dq_out(g, d).wait()
+        for n in range(heads - 1):
+            grad_in(g, n).wait_send()
+            dq_out(g, n, peers[n]).wait()
             for c in range(2):
-                dkv_out(g, c, d).wait()
+                dkv_out(g, c, n, peers[n]).wait()
         dq_own(g).wait()
         for c in range(2):
             dkv_own(g, c).wait()
@@ -322,6 +333,17 @@
         return 0
 
     lax.fori_loop(0, groups, drain, 0)
+
+
+def write_out(dq, dk, dv, dq_hbm, dk_hbm, dv_hbm, sem):
+    copies = [
+        pltpu.make_async_copy(src, dst, sem.at[n])
+        for n, (src, dst) in enumerate(((dq, dq_hbm), (dk, dk_hbm), (dv, dv_hbm)))
+    ]
+    for copy in copies:
+        copy.start()
+    for copy in copies:
+        copy.wait()
 
 
 def on_device(seqs, heads, queries, key_states, value_states, outputs, out_grad, log_norm):
@@ -332,15 +354,16 @@
     low, wide = jnp.bfloat16, jnp.float32
     dma = pltpu.SemaphoreType.DMA
     pairs = groups * ratio * tokens * (WINDOW + BLOCK)
-    return pl.pallas_call(
+    shapes = [
+        (owned, out_grad.shape[1]),
+        (owned, key_states.shape[1] * heads),
+        (owned, key_states.shape[1] * heads),
+    ]
+    landed = pl.pallas_call(
         functools.partial(kernel, seqs, heads, groups, ratio, tokens),
-        out_shape=(
-            jax.ShapeDtypeStruct((owned, out_grad.shape[1]), low),
-            jax.ShapeDtypeStruct((owned, key_states.shape[1] * heads), low),
-            jax.ShapeDtypeStruct((owned, key_states.shape[1] * heads), low),
-        ),
-        in_specs=[pl.BlockSpec(memory_space=pl.ANY)] * 6,
-        out_specs=[pl.BlockSpec(memory_space=pl.ANY)] * 3,
+        out_shape=[pltpu.VMEM(shape, low) for shape in shapes],
+        in_specs=[pl.BlockSpec(memory_space=pltpu.HBM)] * 6,
+        out_specs=[pl.BlockSpec(memory_space=pltpu.VMEM)] * 3,
         scratch_shapes=[
             pltpu.VMEM((groups, tokens, pair), low),
             pltpu.VMEM((groups, tokens, pair), low),
@@ -372,9 +395,16 @@
             flops=10 * pairs * HEAD_DIM, bytes_accessed=12 * tokens * 1024, transcendentals=pairs
         ),
         compiler_params=pltpu.CompilerParams(
-            collective_id=0, has_side_effects=True, vmem_limit_bytes=56 * 1024 * 1024
+            collective_id=0, has_side_effects=True, vmem_limit_bytes=52 * 1024 * 1024
         ),
     )(queries, key_states, value_states, outputs, out_grad, log_norm)
+    return pl.pallas_call(
+        write_out,
+        out_shape=[jax.ShapeDtypeStruct(shape, low) for shape in shapes],
+        in_specs=[pl.BlockSpec(memory_space=pltpu.VMEM)] * 3,
+        out_specs=[pl.BlockSpec(memory_space=pltpu.HBM)] * 3,
+        scratch_shapes=[dma((3,))],
+    )(*landed)
 
 
 def solution(mesh):

time: 149 us -> 149 us (level)
  local copies, waits for them, and re-layouts: 5.79 us -> 3.31 us
  Pallas kernels: 143 us -> 145 us
    pallas_call x0 -> x1, Pallas kernels: none -> 4.2 us  [on_device(): pl.pallas_call(write_out, out_shape=[jax.ShapeDtypeStruct(shape, low) for...]
    unnamed x7 -> x6, local copies, waits for them, and re-layouts: 5.79 us -> 3.31 us
    pallas_call x1, Pallas kernels: 143 us -> 141 us  [on_device(): pl.pallas_call(functools.partial(kernel, seqs, heads, groups, ratio, toke...]
where the time goes in v2:
time: 149 us
  Pallas kernels  145 us (97%)
  local copies, waits for them, and re-layouts  3.31 us (2%)
    pallas_call x1, Pallas kernels, on_device(): pl.pallas_call(functools.partial(kernel, seqs, heads, groups, ratio, toke...  141 us
    pallas_call x1, Pallas kernels, on_device(): pl.pallas_call(write_out, out_shape=[jax.ShapeDtypeStruct(shape, low) for...  4.2 us
    unnamed x6, local copies, waits for them, and re-layouts  3.31 us

profile of v2, /device:TPU:0, one launch (start us, length us, event | category | flops | bytes accessed | tf_op | source)
XLA Modules:
  0.0 149.3 jit_solution(9470244398943335789)
XLA Ops:
  0.6 141.2 %shard_map.85 = (bf16[256,4096]{1,0:T(8,128)(2,1)S(1)}, bf16[256,2048]{1,0:T(8,128)(2,1)S(1)}, bf16[256,2048]{1,0:T(8,128)(2,1)S(1)}) custom-call(bf16[1024,1024]{1,0:T(8,128)(2,1)} %q_hbm.1, bf16[1024,512]{1,0:T(8,128)(2,1)} %k_hbm.1, bf16[1024,512]{1,0:T(8,128)(2,1)} %v_hbm.1, bf16[1024,1024]{1,0:T(8,128)(2,1)} %o_hbm.1, bf16[256,4096]{1,0:T(8,128)(2,1)} %g_hbm.1, ...), custom_call_target="tpu_custom_call" | custom-call | flops 13421772800 | bytes 12582912 | tf_op jit(solution)/shard_map/pallas_call | solution.py:362
  141.8 0.0 copy-start
  141.8 1.3 copy-done
  143.2 0.0 copy-start.1
  143.2 1.0 copy-done.1
  144.2 0.0 copy-start.2
  144.2 1.0 copy-done.2
  145.1 4.2 %shard_map.86 = (bf16[256,4096]{1,0:T(8,128)(2,1)}, bf16[256,2048]{1,0:T(8,128)(2,1)}, bf16[256,2048]{1,0:T(8,128)(2,1)}) custom-call(bf16[256,4096]{1,0:T(8,128)(2,1)} %copy-done, bf16[256,2048]{1,0:T(8,128)(2,1)} %copy-done.1, bf16[256,2048]{1,0:T(8,128)(2,1)} %copy-done.2), custom_call_target="tpu_custom_call" | custom-call | tf_op jit(solution)/shard_map/pallas_call | solution.py:401
Async XLA Ops:
  141.8 1.3 copy-start
  143.2 1.0 copy-start.1
  144.2 1.0 copy-start.2

commit v3 on v2

--- a/solution.py
+++ b/solution.py
@@ -11,7 +11,7 @@
 HEAD_DIM = 128
 WINDOW = 1024
 BLOCK = 256
-AHEAD = 2
+AHEAD = 3
 
 score_scale = 168.0 ** (-0.5)
 LOG2E = math.log2(math.e)
@@ -336,10 +336,12 @@
 
 
 def write_out(dq, dk, dv, dq_hbm, dk_hbm, dv_hbm, sem):
-    copies = [
-        pltpu.make_async_copy(src, dst, sem.at[n])
-        for n, (src, dst) in enumerate(((dq, dq_hbm), (dk, dk_hbm), (dv, dv_hbm)))
-    ]
+    copies = []
+    for src, dst, parts in ((dq, dq_hbm, 4), (dk, dk_hbm, 2), (dv, dv_hbm, 2)):
+        size = src.shape[0] // parts
+        for n in range(parts):
+            rows = pl.ds(n * size, size)
+            copies.append(pltpu.make_async_copy(src.at[rows], dst.at[rows], sem.at[len(copies)]))
     for copy in copies:
         copy.start()
     for copy in copies:
@@ -401,9 +403,10 @@
     return pl.pallas_call(
         write_out,
         out_shape=[jax.ShapeDtypeStruct(shape, low) for shape in shapes],
-        in_specs=[pl.BlockSpec(memory_space=pltpu.VMEM)] * 3,
+        in_specs=[pl.BlockSpec(memory_space=pl.ANY)] * 3,
         out_specs=[pl.BlockSpec(memory_space=pltpu.HBM)] * 3,
-        scratch_shapes=[dma((3,))],
+        scratch_shapes=[dma((8,))],
+        compiler_params=pltpu.CompilerParams(vmem_limit_bytes=1024 * 1024),
     )(*landed)
 
 

time: 149 us -> 144 us (0.966)
  local copies, waits for them, and re-layouts: 3.31 us -> 0 us
  Pallas kernels: 145 us -> 143 us
    unnamed x6 -> x0, local copies, waits for them, and re-layouts: 3.31 us -> none
    pallas_call x1, Pallas kernels: 4.2 us -> 2.07 us  [on_device(): pl.pallas_call(write_out, out_shape=[jax.ShapeDtypeStruct(shape, low) for...]
where the time goes in v3:
time: 144 us
  Pallas kernels  143 us (99%)
    pallas_call x1, Pallas kernels, on_device(): pl.pallas_call(functools.partial(kernel, seqs, heads, groups, ratio, toke...  141 us

profile of v3, /device:TPU:0, one launch (start us, length us, event | category | flops | bytes accessed | tf_op | source)
XLA Modules:
  0.0 144.0 jit_solution(6026894515692037736)
XLA Ops:
  0.6 141.3 %shard_map.85 = (bf16[256,4096]{1,0:T(8,128)(2,1)S(1)}, bf16[256,2048]{1,0:T(8,128)(2,1)S(1)}, bf16[256,2048]{1,0:T(8,128)(2,1)S(1)}) custom-call(bf16[1024,1024]{1,0:T(8,128)(2,1)} %q_hbm.1, bf16[1024,512]{1,0:T(8,128)(2,1)} %k_hbm.1, bf16[1024,512]{1,0:T(8,128)(2,1)} %v_hbm.1, bf16[1024,1024]{1,0:T(8,128)(2,1)} %o_hbm.1, bf16[256,4096]{1,0:T(8,128)(2,1)} %g_hbm.1, ...), custom_call_target="tpu_custom_call" | custom-call | flops 13421772800 | bytes 12582912 | tf_op jit(solution)/shard_map/pallas_call | solution.py:364
  141.9 2.1 %shard_map.86 = (bf16[256,4096]{1,0:T(8,128)(2,1)}, bf16[256,2048]{1,0:T(8,128)(2,1)}, bf16[256,2048]{1,0:T(8,128)(2,1)}) custom-call(bf16[256,4096]{1,0:T(8,128)(2,1)S(1)} %get-tuple-element.6.dq, bf16[256,2048]{1,0:T(8,128)(2,1)S(1)} %get-tuple-element.7.dk, bf16[256,2048]{1,0:T(8,128)(2,1)S(1)} %get-tuple-element.8.dv), custom_call_target="tpu_custom_call" | custom-call | tf_op jit(solution)/shard_map/pallas_call | solution.py:403

commit v4 on v3

--- a/solution.py
+++ b/solution.py
@@ -29,10 +29,10 @@
 def kernel(
     seqs, heads, groups, ratio, tokens,
     q_hbm, k_hbm, v_hbm, o_hbm, g_hbm, n_hbm,
-    dq_hbm, dk_hbm, dv_hbm,
+    dq_land, dkv_land,
     q_buf, o_buf, g_buf, k_ext, v_ext, norm, stats, k_turned, dq_turned,
-    sums, rims, dq_buf, dkv_buf,
-    in_sem, norm_sem, g_send, g_recv, kv_send, kv_recv, rim_send, rim_recv,
+    sums, rims, dq_buf, dkv_buf, staged,
+    in_sem, norm_sem, stage_sem, g_send, g_recv, kv_send, kv_recv, rim_send, rim_recv,
     dq_send, dq_recv, dkv_send, dkv_recv,
 ):
     s, z = lax.axis_index("seq"), lax.axis_index("head")
@@ -67,14 +67,20 @@
             ),
         ]
 
+    def stage(g, n):
+        return pltpu.make_async_copy(
+            g_hbm.at[:, at(peers[n] * groups * pair + g * pair, pair)],
+            staged.at[g, n],
+            stage_sem.at[g, n],
+        )
+
     def grad_in(g, n, source=None):
-        peer = peers[n]
         return pltpu.make_async_remote_copy(
-            src_ref=g_hbm.at[:, at(peer * groups * pair + g * pair, pair)],
+            src_ref=staged.at[g, n],
             dst_ref=g_buf.at[g, at(z * owned, owned)],
             send_sem=g_send.at[g, n],
             recv_sem=g_recv.at[g, z if source is None else source],
-            device_id={"head": peer},
+            device_id={"head": peers[n]},
             device_id_type=MESH,
         )
 
@@ -100,43 +106,38 @@
         )
 
     def dq_out(g, n, source=None):
-        peer = peers[n]
         return pltpu.make_async_remote_copy(
-            src_ref=dq_buf.at[g, at(peer * owned, owned)],
-            dst_ref=dq_hbm.at[:, at(z * groups * pair + g * pair, pair)],
+            src_ref=dq_buf.at[g, at(peers[n] * owned, owned)],
+            dst_ref=dq_land.at[z * groups + g],
             send_sem=dq_send.at[g, n],
             recv_sem=dq_recv.at[g, z if source is None else source],
-            device_id={"head": peer},
+            device_id={"head": peers[n]},
             device_id_type=MESH,
         )
 
     def dq_own(g):
         return pltpu.make_async_copy(
-            dq_buf.at[g, at(z * owned, owned)],
-            dq_hbm.at[:, at(z * groups * pair + g * pair, pair)],
-            dq_send.at[g, mine],
-        )
-
-    def dkv_out(g, c, n, source=None):
-        peer = peers[n]
+            dq_buf.at[g, at(z * owned, owned)], dq_land.at[z * groups + g], dq_send.at[g, mine]
+        )
+
+    def dkv_out(g, n, source=None):
         return pltpu.make_async_remote_copy(
-            src_ref=dkv_buf.at[g, c, at(peer * owned, owned)],
-            dst_ref=(dk_hbm, dv_hbm)[c].at[:, at((z * groups + g) * HEAD_DIM, HEAD_DIM)],
-            send_sem=dkv_send.at[g, c, n],
-            recv_sem=dkv_recv.at[g, c, z if source is None else source],
-            device_id={"head": peer},
+            src_ref=dkv_buf.at[g, peers[n]],
+            dst_ref=dkv_land.at[z * groups + g],
+            send_sem=dkv_send.at[g, n],
+            recv_sem=dkv_recv.at[g, z if source is None else source],
+            device_id={"head": peers[n]},
             device_id_type=MESH,
         )
 
-    def dkv_own(g, c):
+    def dkv_own(g):
         return pltpu.make_async_copy(
-            dkv_buf.at[g, c, at(z * owned, owned)],
-            (dk_hbm, dv_hbm)[c].at[:, at((z * groups + g) * HEAD_DIM, HEAD_DIM)],
-            dkv_send.at[g, c, mine],
+            dkv_buf.at[g, z], dkv_land.at[z * groups + g], dkv_send.at[g, mine]
         )
 
     def send_grads(g):
         for n in range(heads - 1):
+            stage(g, n).wait()
             grad_in(g, n).start()
 
     def send_windows(g):
@@ -232,28 +233,16 @@
 
             lax.fori_loop(0, rim_blocks, add, 0)
 
-        def rows_of(i, _):
-            rows, own = at(i * BLOCK, BLOCK), at(WINDOW + i * BLOCK, BLOCK)
-            dkv_buf[g, 0, rows, :] = (sums[g, 0, own, :] * score_scale).astype(jnp.bfloat16)
-            dkv_buf[g, 1, rows, :] = sums[g, 1, own, :].astype(jnp.bfloat16)
+        def owner_of(n, _):
+            own = at(WINDOW + n * owned, owned)
+            dkv_buf[g, n, 0] = (sums[g, 0, own, :] * score_scale).astype(jnp.bfloat16)
+            dkv_buf[g, n, 1] = sums[g, 1, own, :].astype(jnp.bfloat16)
             return 0
 
-        lax.fori_loop(0, q_blocks, rows_of, 0)
-        for n in range(heads - 1):
-            for c in range(2):
-                dkv_out(g, c, n).start()
-        for c in range(2):
-            dkv_own(g, c).start()
-
-    norm_in = pltpu.make_async_copy(n_hbm, norm, norm_sem)
-    norm_in.start()
-
-    def start_inputs(g, _):
-        for copy in inputs(g):
-            copy.start()
-        return 0
-
-    lax.fori_loop(0, groups, start_inputs, 0)
+        lax.fori_loop(0, heads, owner_of, 0)
+        for n in range(heads - 1):
+            dkv_out(g, n).start()
+        dkv_own(g).start()
 
     barrier = pltpu.get_barrier_semaphore()
     for d in range(1, heads):
@@ -269,6 +258,17 @@
     def _():
         pl.semaphore_signal(barrier, inc=1, device_id={"seq": s + 1}, device_id_type=MESH)
 
+    def start_stage(g, _):
+        for n in range(heads - 1):
+            stage(g, n).start()
+        return 0
+
+    lax.fori_loop(0, groups, start_stage, 0)
+    norm_in = pltpu.make_async_copy(n_hbm, norm, norm_sem)
+    norm_in.start()
+    for copy in inputs(0):
+        copy.start()
+
     pl.semaphore_wait(
         barrier, heads - 1 + has_before.astype(jnp.int32) + has_after.astype(jnp.int32)
     )
@@ -279,6 +279,11 @@
     norm_in.wait()
 
     def one_group(g, _):
+        @pl.when(g + 1 < groups)
+        def _():
+            for copy in inputs(g + 1):
+                copy.start()
+
         for copy in inputs(g):
             copy.wait()
         for n in range(heads - 1):
@@ -315,11 +320,9 @@
         for n in range(heads - 1):
             grad_in(g, n).wait_send()
             dq_out(g, n, peers[n]).wait()
-            for c in range(2):
-                dkv_out(g, c, n, peers[n]).wait()
+            dkv_out(g, n, peers[n]).wait()
         dq_own(g).wait()
-        for c in range(2):
-            dkv_own(g, c).wait()
+        dkv_own(g).wait()
 
         @pl.when(has_after)
         def _():
@@ -335,17 +338,23 @@
     lax.fori_loop(0, groups, drain, 0)
 
 
-def write_out(dq, dk, dv, dq_hbm, dk_hbm, dv_hbm, sem):
-    copies = []
-    for src, dst, parts in ((dq, dq_hbm, 4), (dk, dk_hbm, 2), (dv, dv_hbm, 2)):
-        size = src.shape[0] // parts
-        for n in range(parts):
-            rows = pl.ds(n * size, size)
-            copies.append(pltpu.make_async_copy(src.at[rows], dst.at[rows], sem.at[len(copies)]))
-    for copy in copies:
-        copy.start()
-    for copy in copies:
-        copy.wait()
+def write_out(dq_land, dkv_land, dq_hbm, dk_hbm, dv_hbm, sem):
+    blocks, _, pair = dq_land.shape
+
+    def copies(n):
+        narrow = at(n * HEAD_DIM, HEAD_DIM)
+        return [
+            pltpu.make_async_copy(dq_land.at[n], dq_hbm.at[:, at(n * pair, pair)], sem.at[n, 0]),
+            pltpu.make_async_copy(dkv_land.at[n, 0], dk_hbm.at[:, narrow], sem.at[n, 1]),
+            pltpu.make_async_copy(dkv_land.at[n, 1], dv_hbm.at[:, narrow], sem.at[n, 2]),
+        ]
+
+    for n in range(blocks):
+        for copy in copies(n):
+            copy.start()
+    for n in range(blocks):
+        for copy in copies(n):
+            copy.wait()
 
 
 def on_device(seqs, heads, queries, key_states, value_states, outputs, out_grad, log_norm):
@@ -363,9 +372,12 @@
     ]
     landed = pl.pallas_call(
         functools.partial(kernel, seqs, heads, groups, ratio, tokens),
-        out_shape=[pltpu.VMEM(shape, low) for shape in shapes],
+        out_shape=[
+            pltpu.VMEM((heads * groups, owned, pair), low),
+            pltpu.VMEM((heads * groups, 2, owned, HEAD_DIM), low),
+        ],
         in_specs=[pl.BlockSpec(memory_space=pltpu.HBM)] * 6,
-        out_specs=[pl.BlockSpec(memory_space=pltpu.VMEM)] * 3,
+        out_specs=[pl.BlockSpec(memory_space=pltpu.VMEM)] * 2,
         scratch_shapes=[
             pltpu.VMEM((groups, tokens, pair), low),
             pltpu.VMEM((groups, tokens, pair), low),
@@ -379,9 +391,11 @@
             pltpu.VMEM((groups, 2, span, HEAD_DIM), wide),
             pltpu.VMEM((groups, 2, WINDOW, HEAD_DIM), wide),
             pltpu.VMEM((groups, tokens, pair), low),
-            pltpu.VMEM((groups, 2, tokens, HEAD_DIM), low),
+            pltpu.VMEM((groups, heads, 2, owned, HEAD_DIM), low),
+            pltpu.VMEM((groups, heads - 1, owned, pair), low),
             dma((groups, 5)),
             dma,
+            dma((groups, heads)),
             dma((groups, heads)),
             dma((groups, heads)),
             dma((groups, 2)),
@@ -390,8 +404,8 @@
             dma((groups,)),
             dma((groups, heads)),
             dma((groups, heads)),
-            dma((groups, 2, heads)),
-            dma((groups, 2, heads)),
+            dma((groups, heads)),
+            dma((groups, heads)),
         ],
         cost_estimate=pl.CostEstimate(
             flops=10 * pairs * HEAD_DIM, bytes_accessed=12 * tokens * 1024, transcendentals=pairs
@@ -403,9 +417,9 @@
     return pl.pallas_call(
         write_out,
         out_shape=[jax.ShapeDtypeStruct(shape, low) for shape in shapes],
-        in_specs=[pl.BlockSpec(memory_space=pl.ANY)] * 3,
+        in_specs=[pl.BlockSpec(memory_space=pl.ANY)] * 2,
         out_specs=[pl.BlockSpec(memory_space=pltpu.HBM)] * 3,
-        scratch_shapes=[dma((8,))],
+        scratch_shapes=[dma((heads * groups, 3))],
         compiler_params=pltpu.CompilerParams(vmem_limit_bytes=1024 * 1024),
     )(*landed)
 

time: 144 us -> 144 us (level)
  no operation moved by 1% of the time
where the time goes in v4:
time: 144 us
  Pallas kernels  143 us (99%)
    pallas_call x1, Pallas kernels, on_device(): pl.pallas_call(functools.partial(kernel, seqs, heads, groups, ratio, toke...  141 us

profile of v4, /device:TPU:0, one launch (start us, length us, event | category | flops | bytes accessed | tf_op | source)
XLA Modules:
  0.0 143.9 jit_solution(12313376026048881275)
XLA Ops:
  0.6 140.9 %shard_map.85 = (bf16[16,256,256]{2,1,0:T(8,128)(2,1)S(1)}, bf16[16,2,256,128]{3,2,1,0:T(8,128)(2,1)S(1)}) custom-call(bf16[1024,1024]{1,0:T(8,128)(2,1)} %q_hbm.1, bf16[1024,512]{1,0:T(8,128)(2,1)} %k_hbm.1, bf16[1024,512]{1,0:T(8,128)(2,1)} %v_hbm.1, bf16[1024,1024]{1,0:T(8,128)(2,1)} %o_hbm.1, bf16[256,4096]{1,0:T(8,128)(2,1)} %g_hbm.1, f32[8,1024]{1,0:T(8,128)} %n_hbm.1), custom_call_target="tpu_custom_call" | custom-call | flops 13421772800 | bytes 12582912 | tf_op jit(solution)/shard_map/pallas_call | solution.py:373
  141.5 2.4 %shard_map.86 = (bf16[256,4096]{1,0:T(8,128)(2,1)}, bf16[256,2048]{1,0:T(8,128)(2,1)}, bf16[256,2048]{1,0:T(8,128)(2,1)}) custom-call(bf16[16,256,256]{2,1,0:T(8,128)(2,1)S(1)} %get-tuple-element.5.dq_land, bf16[16,2,256,128]{3,2,1,0:T(8,128)(2,1)S(1)} %get-tuple-element.6.dkv_land), custom_call_target="tpu_custom_call" | custom-call | tf_op jit(solution)/shard_map/pallas_call | solution.py:417

commit v5 on v4

--- a/solution.py
+++ b/solution.py
@@ -31,7 +31,7 @@
     q_hbm, k_hbm, v_hbm, o_hbm, g_hbm, n_hbm,
     dq_land, dkv_land,
     q_buf, o_buf, g_buf, k_ext, v_ext, norm, stats, k_turned, dq_turned,
-    sums, rims, dq_buf, dkv_buf, staged,
+    sums, rim_low, rims, dq_buf, dkv_buf, staged,
     in_sem, norm_sem, stage_sem, g_send, g_recv, kv_send, kv_recv, rim_send, rim_recv,
     dq_send, dq_recv, dkv_send, dkv_recv,
 ):
@@ -41,12 +41,18 @@
     q_blocks, rim_blocks = tokens // BLOCK, WINDOW // BLOCK
     has_before, has_after = s > 0, s < seqs - 1
 
-    in_low = (2 * z < heads).astype(jnp.int32)
+    half = heads // 2
+    in_low = (z < half).astype(jnp.int32)
 
     def peer_of(n):
-        down, up = heads - 1 - n, jnp.int32(n)
-        down -= (down <= z).astype(jnp.int32)
-        up += (up >= z).astype(jnp.int32)
+        if heads % 2:
+            return lax.rem(z + 1 + n, heads)
+        if n < half:
+            down = heads - 1 - lax.rem(z + n, half)
+            up = lax.rem(heads - 1 - z + n, half)
+        else:
+            down = lax.rem(z + 1 + n - half, half)
+            up = half + lax.rem(z + 1 + n - half, half)
         return in_low * down + (1 - in_low) * up
 
     peers = [peer_of(n) for n in range(heads - 1)]
@@ -97,7 +103,7 @@
 
     def rim_out(g):
         return pltpu.make_async_remote_copy(
-            src_ref=sums.at[g, :, pl.ds(0, WINDOW)],
+            src_ref=rim_low.at[g],
             dst_ref=rims.at[g],
             send_sem=rim_send.at[g],
             recv_sem=rim_recv.at[g],
@@ -183,6 +189,8 @@
         sums[g, :, keys, :] = jnp.zeros((2, BLOCK, HEAD_DIM), jnp.float32)
         low, high = jnp.maximum(j - rim_blocks, 0), jnp.minimum(j + 1, q_blocks)
         lax.fori_loop(low, high, lambda i, _: (tile(g, j, i, in_rim), 0)[1], 0)
+        if in_rim:
+            rim_low[g, :, keys, :] = sums[g, :, keys, :].astype(jnp.bfloat16)
 
     def prepare(g):
         ones = jnp.ones((8, HEAD_DIM), jnp.bfloat16)
@@ -228,7 +236,7 @@
                 rows = at(i * BLOCK, BLOCK)
                 own = at(tokens + i * BLOCK, BLOCK)
                 for c in range(2):
-                    sums[g, c, own, :] += rims[g, c, rows, :]
+                    sums[g, c, own, :] += rims[g, c, rows, :].astype(jnp.float32)
                 return 0
 
             lax.fori_loop(0, rim_blocks, add, 0)
@@ -389,7 +397,8 @@
             pltpu.VMEM((HEAD_DIM, span), low),
             pltpu.VMEM((ratio, HEAD_DIM, tokens), wide),
             pltpu.VMEM((groups, 2, span, HEAD_DIM), wide),
-            pltpu.VMEM((groups, 2, WINDOW, HEAD_DIM), wide),
+            pltpu.VMEM((groups, 2, WINDOW, HEAD_DIM), low),
+            pltpu.VMEM((groups, 2, WINDOW, HEAD_DIM), low),
             pltpu.VMEM((groups, tokens, pair), low),
             pltpu.VMEM((groups, heads, 2, owned, HEAD_DIM), low),
             pltpu.VMEM((groups, heads - 1, owned, pair), low),

time: 144 us -> 146 us (1.014)
  Pallas kernels: 143 us -> 145 us
    pallas_call x1, Pallas kernels: 141 us -> 143 us  [on_device(): pl.pallas_call(functools.partial(kernel, seqs, heads, groups, ratio, toke...]
where the time goes in v5:
time: 146 us
  Pallas kernels  145 us (99%)
    pallas_call x1, Pallas kernels, on_device(): pl.pallas_call(functools.partial(kernel, seqs, heads, groups, ratio, toke...  143 us

profile of v5, /device:TPU:0, one launch (start us, length us, event | category | flops | bytes accessed | tf_op | source)
XLA Modules:
  0.0 146.0 jit_solution(8118050977974937558)
XLA Ops:
  0.6 143.0 %shard_map.85 = (bf16[16,256,256]{2,1,0:T(8,128)(2,1)S(1)}, bf16[16,2,256,128]{3,2,1,0:T(8,128)(2,1)S(1)}) custom-call(bf16[1024,1024]{1,0:T(8,128)(2,1)} %q_hbm.1, bf16[1024,512]{1,0:T(8,128)(2,1)} %k_hbm.1, bf16[1024,512]{1,0:T(8,128)(2,1)} %v_hbm.1, bf16[1024,1024]{1,0:T(8,128)(2,1)} %o_hbm.1, bf16[256,4096]{1,0:T(8,128)(2,1)} %g_hbm.1, f32[8,1024]{1,0:T(8,128)} %n_hbm.1), custom_call_target="tpu_custom_call" | custom-call | flops 13421772800 | bytes 12582912 | tf_op jit(solution)/shard_map/pallas_call | solution.py:381
  143.6 2.4 %shard_map.86 = (bf16[256,4096]{1,0:T(8,128)(2,1)}, bf16[256,2048]{1,0:T(8,128)(2,1)}, bf16[256,2048]{1,0:T(8,128)(2,1)}) custom-call(bf16[16,256,256]{2,1,0:T(8,128)(2,1)S(1)} %get-tuple-element.5.dq_land, bf16[16,2,256,128]{3,2,1,0:T(8,128)(2,1)S(1)} %get-tuple-element.6.dkv_land), custom_call_target="tpu_custom_call" | custom-call | tf_op jit(solution)/shard_map/pallas_call | solution.py:426

commit v6 on v4

--- a/solution.py
+++ b/solution.py
@@ -41,13 +41,26 @@
     q_blocks, rim_blocks = tokens // BLOCK, WINDOW // BLOCK
     has_before, has_after = s > 0, s < seqs - 1
 
-    in_low = (2 * z < heads).astype(jnp.int32)
+    half, edge = heads // 2, heads // 4
+    in_low = (z < half).astype(jnp.int32)
+    inner = (z >= edge).astype(jnp.int32) * (z < heads - edge).astype(jnp.int32)
+
+    def same_half(n):
+        return (1 - in_low) * half + lax.rem(z + 1 + n, half)
 
     def peer_of(n):
-        down, up = heads - 1 - n, jnp.int32(n)
-        down -= (down <= z).astype(jnp.int32)
-        up += (up >= z).astype(jnp.int32)
-        return in_low * down + (1 - in_low) * up
+        if heads % 2:
+            return lax.rem(z + 1 + n, heads)
+        if n < half:
+            from_edge = in_low * (half + n) + (1 - in_low) * (half - 1 - n)
+        else:
+            from_edge = same_half(n - half)
+        if n < half - 1:
+            from_inner = same_half(n)
+        else:
+            far = n - (half - 1)
+            from_inner = in_low * (heads - 1 - far) + (1 - in_low) * far
+        return inner * from_inner + (1 - inner) * from_edge
 
     peers = [peer_of(n) for n in range(heads - 1)]
     mine = heads - 1

time: 144 us -> 144 us (level)
  no operation moved by 1% of the time
where the time goes in v6:
time: 144 us
  Pallas kernels  143 us (99%)
    pallas_call x1, Pallas kernels, on_device(): pl.pallas_call(functools.partial(kernel, seqs, heads, groups, ratio, toke...  141 us

profile of v6, /device:TPU:0, one launch (start us, length us, event | category | flops | bytes accessed | tf_op | source)
XLA Modules:
  0.0 144.0 jit_solution(15085607590691293079)
XLA Ops:
  0.6 140.9 %shard_map.85 = (bf16[16,256,256]{2,1,0:T(8,128)(2,1)S(1)}, bf16[16,2,256,128]{3,2,1,0:T(8,128)(2,1)S(1)}) custom-call(bf16[1024,1024]{1,0:T(8,128)(2,1)} %q_hbm.1, bf16[1024,512]{1,0:T(8,128)(2,1)} %k_hbm.1, bf16[1024,512]{1,0:T(8,128)(2,1)} %v_hbm.1, bf16[1024,1024]{1,0:T(8,128)(2,1)} %o_hbm.1, bf16[256,4096]{1,0:T(8,128)(2,1)} %g_hbm.1, f32[8,1024]{1,0:T(8,128)} %n_hbm.1), custom_call_target="tpu_custom_call" | custom-call | flops 13421772800 | bytes 12582912 | tf_op jit(solution)/shard_map/pallas_call | solution.py:386
  141.6 2.4 %shard_map.86 = (bf16[256,4096]{1,0:T(8,128)(2,1)}, bf16[256,2048]{1,0:T(8,128)(2,1)}, bf16[256,2048]{1,0:T(8,128)(2,1)}) custom-call(bf16[16,256,256]{2,1,0:T(8,128)(2,1)S(1)} %get-tuple-element.5.dq_land, bf16[16,2,256,128]{3,2,1,0:T(8,128)(2,1)S(1)} %get-tuple-element.6.dkv_land), custom_call_target="tpu_custom_call" | custom-call | tf_op jit(solution)/shard_map/pallas_call | solution.py:430

commit v7 on v6

--- a/solution.py
+++ b/solution.py
@@ -31,7 +31,7 @@
     q_hbm, k_hbm, v_hbm, o_hbm, g_hbm, n_hbm,
     dq_land, dkv_land,
     q_buf, o_buf, g_buf, k_ext, v_ext, norm, stats, k_turned, dq_turned,
-    sums, rims, dq_buf, dkv_buf, staged,
+    sums, rim_low, rims, dq_buf, dkv_buf, staged,
     in_sem, norm_sem, stage_sem, g_send, g_recv, kv_send, kv_recv, rim_send, rim_recv,
     dq_send, dq_recv, dkv_send, dkv_recv,
 ):
@@ -110,7 +110,7 @@
 
     def rim_out(g):
         return pltpu.make_async_remote_copy(
-            src_ref=sums.at[g, :, pl.ds(0, WINDOW)],
+            src_ref=rim_low.at[g],
             dst_ref=rims.at[g],
             send_sem=rim_send.at[g],
             recv_sem=rim_recv.at[g],
@@ -196,6 +196,8 @@
         sums[g, :, keys, :] = jnp.zeros((2, BLOCK, HEAD_DIM), jnp.float32)
         low, high = jnp.maximum(j - rim_blocks, 0), jnp.minimum(j + 1, q_blocks)
         lax.fori_loop(low, high, lambda i, _: (tile(g, j, i, in_rim), 0)[1], 0)
+        if in_rim:
+            rim_low[g, :, keys, :] = sums[g, :, keys, :].astype(jnp.bfloat16)
 
     def prepare(g):
         ones = jnp.ones((8, HEAD_DIM), jnp.bfloat16)
@@ -241,7 +243,7 @@
                 rows = at(i * BLOCK, BLOCK)
                 own = at(tokens + i * BLOCK, BLOCK)
                 for c in range(2):
-                    sums[g, c, own, :] += rims[g, c, rows, :]
+                    sums[g, c, own, :] += rims[g, c, rows, :].astype(jnp.float32)
                 return 0
 
             lax.fori_loop(0, rim_blocks, add, 0)
@@ -402,7 +404,8 @@
             pltpu.VMEM((HEAD_DIM, span), low),
             pltpu.VMEM((ratio, HEAD_DIM, tokens), wide),
             pltpu.VMEM((groups, 2, span, HEAD_DIM), wide),
-            pltpu.VMEM((groups, 2, WINDOW, HEAD_DIM), wide),
+            pltpu.VMEM((groups, 2, WINDOW, HEAD_DIM), low),
+            pltpu.VMEM((groups, 2, WINDOW, HEAD_DIM), low),
             pltpu.VMEM((groups, tokens, pair), low),
             pltpu.VMEM((groups, heads, 2, owned, HEAD_DIM), low),
             pltpu.VMEM((groups, heads - 1, owned, pair), low),

time: 144 us -> 144 us (level)
  no operation moved by 1% of the time
where the time goes in v7:
time: 144 us
  Pallas kernels  143 us (99%)
    pallas_call x1, Pallas kernels, on_device(): pl.pallas_call(functools.partial(kernel, seqs, heads, groups, ratio, toke...  141 us

profile of v7, /device:TPU:0, one launch (start us, length us, event | category | flops | bytes accessed | tf_op | source)
XLA Modules:
  0.0 144.0 jit_solution(11274736939256546329)
XLA Ops:
  0.6 141.0 %shard_map.85 = (bf16[16,256,256]{2,1,0:T(8,128)(2,1)S(1)}, bf16[16,2,256,128]{3,2,1,0:T(8,128)(2,1)S(1)}) custom-call(bf16[1024,1024]{1,0:T(8,128)(2,1)} %q_hbm.1, bf16[1024,512]{1,0:T(8,128)(2,1)} %k_hbm.1, bf16[1024,512]{1,0:T(8,128)(2,1)} %v_hbm.1, bf16[1024,1024]{1,0:T(8,128)(2,1)} %o_hbm.1, bf16[256,4096]{1,0:T(8,128)(2,1)} %g_hbm.1, f32[8,1024]{1,0:T(8,128)} %n_hbm.1), custom_call_target="tpu_custom_call" | custom-call | flops 13421772800 | bytes 12582912 | tf_op jit(solution)/shard_map/pallas_call | solution.py:388
  141.6 2.4 %shard_map.86 = (bf16[256,4096]{1,0:T(8,128)(2,1)}, bf16[256,2048]{1,0:T(8,128)(2,1)}, bf16[256,2048]{1,0:T(8,128)(2,1)}) custom-call(bf16[16,256,256]{2,1,0:T(8,128)(2,1)S(1)} %get-tuple-element.5.dq_land, bf16[16,2,256,128]{3,2,1,0:T(8,128)(2,1)S(1)} %get-tuple-element.6.dkv_land), custom_call_target="tpu_custom_call" | custom-call | tf_op jit(solution)/shard_map/pallas_call | solution.py:433
